TPU v7x, 32 devices: a whole 2x2x4 slice. The times are simulated.
32 devices in a mesh: rep: 8 (over y, x, core), shard: 4 (over z).
Axes of the slice: x: 2, y: 2, z: 4, core: 2. Of those that a mesh axis runs over, the one named last changes fastest.
Arguments:
- tokens: bfloat16 [16384, 1024], P(('rep', 'shard')), may hold values from -6 to 6
- doc_ids: int32 [16384], P(('rep', 'shard')), may hold values from 0 to 511, as said below
- routes: int32 [16384, 8], P(('rep', 'shard')), may hold values from 0 to 15, all different within a row; in each aligned block of 512 rows (0 to 511, 512 to 1023, ...) at most 288 rows name the same one
- norm_in_gain: bfloat16 [1024], P('shard'), may hold values from 0.5 to 1.5
- w_query: bfloat16 [1024, 1024], P('shard'), may hold values from -0.1875 to 0.1875
- w_key: bfloat16 [1024, 512], P('shard'), may hold values from -0.1875 to 0.1875
- w_value: bfloat16 [1024, 512], P('shard'), may hold values from -0.1875 to 0.1875
- w_out: bfloat16 [1024, 1024], P('shard'), may hold values from -0.75 to 0.75
- norm_mid_gain: bfloat16 [1024], P('shard'), may hold values from 0.5 to 1.5
- w_router: bfloat16 [1024, 16], P('shard'), may hold values from -0.09375 to 0.09375
- w_expert_in: bfloat16 [16, 1024, 1024], P('shard'), may hold values from -0.1875 to 0.1875
- w_expert_down: bfloat16 [16, 512, 1024], P('shard'), may hold values from -0.75 to 0.75
- cotangent: bfloat16 [16384, 1024], P(('rep', 'shard')), may hold values from -6 to 6
Outputs:
- mixed: bfloat16 [16384, 1024], P(('rep', 'shard'))
- grad_tokens: float32 [16384, 1024], P(('rep', 'shard'))
- grad_norm_in_gain: float32 [1024], P('shard')
- grad_w_query: float32 [1024, 1024], P('shard')
- grad_w_key: float32 [1024, 512], P('shard')
- grad_w_value: float32 [1024, 512], P('shard')
- grad_w_out: float32 [1024, 1024], P('shard')
- grad_norm_mid_gain: float32 [1024], P('shard')
- grad_w_router: float32 [1024, 16], P('shard')
- grad_w_expert_in: float32 [16, 1024, 1024], P('shard')
- grad_w_expert_down: float32 [16, 512, 1024], P('shard')
Inputs may be any that keep to these rules, and one draw needn't show every extreme that they name: `doc_ids`: in every aligned block of 512 tokens the numbers start at 0 and rise by 0 or 1 from token to token. Among the 512 tokens of one device, no expert is named by more than 288 routes.
All inputs are finite; a program needn't handle non-finite values.
Results may differ from a plain program's by a relative error of at most 0.019.
Values may be sent and summed in bfloat16 or wider, within the bound.
A program may use at most 320 MiB of HBM per device.

v0:
```python
import jax
import jax.numpy as jnp
from jax import lax
from jax.sharding import PartitionSpec as P

HEADS = 16
KV_HEADS = 8
HEAD_DIM = 64
EXPERTS = 16
PAD = 128
epsilon = 1e-06
rope_base = 10000.0
masked_score = -1e30


def positions(doc_rows):
    row_count = doc_rows.shape[0]
    places = jnp.arange(row_count, dtype=jnp.int32)
    opening = jnp.concatenate([jnp.ones((1,), dtype=jnp.bool_), doc_rows[1:] != doc_rows[:-1]])
    begins = lax.cummax(jnp.where(opening, places, 0), axis=0)
    return places - begins


def rotary_tables(places, head_width):
    half_width = head_width // 2
    frequencies = jnp.power(
        rope_base, -2.0 * jnp.arange(half_width, dtype=jnp.float32) / head_width
    )
    angles = places.astype(jnp.float32)[:, None] * frequencies[None, :]
    return (jnp.cos(angles)[:, None, :], jnp.sin(angles)[:, None, :])


def rotate(values, cosine, sine_table):
    half_width = values.shape[-1] // 2
    former, latter = (values[..., :half_width], values[..., half_width:])
    return jnp.concatenate(
        [former * cosine - latter * sine_table, latter * cosine + former * sine_table], axis=-1
    )


def unrotate(values, cosine, sine_table):
    half_width = values.shape[-1] // 2
    former, latter = (values[..., :half_width], values[..., half_width:])
    return jnp.concatenate(
        [former * cosine + latter * sine_table, latter * cosine - former * sine_table], axis=-1
    )


def normalize(values):
    row_scale = lax.rsqrt(jnp.mean(values * values, axis=-1, keepdims=True) + epsilon)
    return (values * row_scale, row_scale)


def norm_back(grad_scaled, normed, row_scale, gain_full):
    grad_normed = grad_scaled * gain_full
    inner = jnp.mean(grad_normed * normed, axis=-1, keepdims=True)
    return (row_scale * (grad_normed - normed * inner), jnp.sum(grad_scaled * normed, axis=0))


def score_block(query_blk, key_part, doc_query, doc_key):
    scores = jnp.einsum(
        "qgrd,kgd->grqk", query_blk, key_part, preferred_element_type=jnp.float32
    ) * query_blk.shape[-1] ** (-0.5)
    query_place = jnp.arange(query_blk.shape[0], dtype=jnp.int32)
    key_place = jnp.arange(key_part.shape[0], dtype=jnp.int32)
    allowed = (doc_query[:, None] == doc_key[None, :]) & (
        query_place[:, None] >= key_place[None, :]
    )
    return jnp.where(allowed, scores, masked_score)


def attend(query_rows, key_rows, value_rows, doc_rows):
    scores = score_block(query_rows, key_rows, doc_rows, doc_rows)
    row_max = jnp.max(scores, axis=-1, keepdims=True)
    exponent = jnp.exp(scores - row_max)
    row_total = jnp.sum(exponent, axis=-1, keepdims=True)
    probs_low = (exponent / row_total).astype(jnp.bfloat16)
    outputs = jnp.einsum(
        "grqk,kgd->qgrd", probs_low, value_rows, preferred_element_type=jnp.float32
    ).astype(jnp.bfloat16)
    lse_parts = row_max + jnp.log(row_total)
    return (outputs, lse_parts)


def attend_back(query_rows, key_rows, value_rows, doc_rows, log_sums, grad_att):
    row_count = query_rows.shape[0]
    block_rows = min(512, row_count)
    scale_factor = query_rows.shape[-1] ** (-0.5)
    grad_key = jnp.zeros(key_rows.shape, jnp.float32)
    grad_value = jnp.zeros(value_rows.shape, jnp.float32)
    scores = score_block(query_rows, key_rows, doc_rows, doc_rows)
    probs = jnp.exp(scores - log_sums)
    grad_probs = jnp.einsum(
        "qgrd,kgd->grqk", grad_att, value_rows, preferred_element_type=jnp.float32
    )
    inner = jnp.sum(probs * grad_probs, axis=-1, keepdims=True)
    grad_scores = (probs * (grad_probs - inner)).astype(jnp.bfloat16)
    query_parts = (
        jnp.einsum("grqk,kgd->qgrd", grad_scores, key_rows, preferred_element_type=jnp.float32)
        * scale_factor
    )
    grad_key = grad_key.at[:block_rows].add(
        jnp.einsum("grqk,qgrd->kgd", grad_scores, query_rows, preferred_element_type=jnp.float32)
        * scale_factor
    )
    grad_value = grad_value.at[:block_rows].add(
        jnp.einsum(
            "grqk,qgrd->kgd",
            probs.astype(jnp.bfloat16),
            grad_att,
            preferred_element_type=jnp.float32,
        )
    )
    return (query_parts, grad_key, grad_value)


def gather_shard(piece):
    return lax.all_gather(piece, "shard", axis=0, tiled=True)


def shards(
    tokens,
    doc_ids,
    routes,
    norm_in_gain,
    w_query,
    w_key,
    w_value,
    w_out,
    norm_mid_gain,
    w_router,
    w_expert_in,
    w_expert_down,
    cotangent,
):
    bf16, f32 = (jnp.bfloat16, jnp.float32)
    row_count, model_width = tokens.shape
    groups = HEADS // KV_HEADS
    query_cols = w_query.shape[1]
    kv_cols = w_key.shape[1]
    own_rows = w_query.shape[0]
    own_experts, ff = w_expert_down.shape[:2]
    shard_at = lax.axis_index("shard")
    small = jnp.concatenate(
        [
            w_router,
            norm_in_gain[:, None],
            norm_mid_gain[:, None],
            jnp.zeros((own_rows, PAD - EXPERTS - 2), bf16),
        ],
        axis=1,
    )
    qkv_full = gather_shard(jnp.concatenate([w_query, w_key, w_value, small], axis=1))
    qkv_w = qkv_full[:, : query_cols + 2 * kv_cols]
    small_full = qkv_full[:, query_cols + 2 * kv_cols :]
    router_full = small_full[:, :EXPERTS]
    gain_in = small_full[:, EXPERTS].astype(f32)
    gain_mid = small_full[:, EXPERTS + 1].astype(f32)
    out_w = gather_shard(w_out)
    mask_own = jnp.any(
        routes[:, :, None] == jnp.arange(EXPERTS, dtype=jnp.int32)[None, None, :], axis=1
    )
    side = jnp.concatenate(
        [cotangent, mask_own.astype(bf16), jnp.zeros((row_count, PAD - EXPERTS), bf16)], axis=1
    )
    side_all = gather_shard(side)
    dy_all = side_all[:, :model_width]
    mask_all = side_all[:, model_width : model_width + EXPERTS] > 0
    inputs = tokens.astype(f32)
    grad_final = cotangent.astype(f32)
    cosine, sine_table = rotary_tables(positions(doc_ids), HEAD_DIM)
    normed_in, scale_in = normalize(inputs)
    first_low = (normed_in * gain_in).astype(bf16)
    qkv_pre = jnp.dot(first_low, qkv_w, preferred_element_type=f32)
    query_pre = qkv_pre[:, :query_cols]
    key_pre = qkv_pre[:, query_cols : query_cols + kv_cols]
    value_pre = qkv_pre[:, query_cols + kv_cols :]
    query_rows = (
        rotate(query_pre.reshape(row_count, HEADS, HEAD_DIM), cosine, sine_table)
        .astype(bf16)
        .reshape(row_count, KV_HEADS, groups, HEAD_DIM)
    )
    key_rows = rotate(key_pre.reshape(row_count, KV_HEADS, HEAD_DIM), cosine, sine_table).astype(
        bf16
    )
    value_rows = value_pre.astype(bf16).reshape(row_count, KV_HEADS, HEAD_DIM)
    att_rows, log_sums = attend(query_rows, key_rows, value_rows, doc_ids)
    att_low = att_rows.reshape(row_count, query_cols)
    middle = inputs + jnp.dot(att_low, out_w, preferred_element_type=f32)
    normed_mid, scale_mid = normalize(middle)
    second_low = (normed_mid * gain_mid).astype(bf16)
    second_all = gather_shard(second_low)
    logits = jnp.dot(second_all, router_full, preferred_element_type=f32)
    chosen = jnp.where(mask_all, logits, masked_score)
    gate_exp = jnp.where(mask_all, jnp.exp(chosen - jnp.max(chosen, axis=1, keepdims=True)), 0.0)
    gates_all = gate_exp / jnp.sum(gate_exp, axis=1, keepdims=True)
    gates_here = lax.dynamic_slice_in_dim(gates_all, shard_at * own_experts, own_experts, axis=1)
    gates_own = lax.dynamic_slice_in_dim(gates_all, shard_at * row_count, row_count, axis=0)
    gated, grad_both, grad_gates_here = experts(
        second_all, dy_all, gates_here, w_expert_in, w_expert_down
    )
    combined = jnp.einsum("etf,efd->td", gated, w_expert_down, preferred_element_type=f32)
    combined_own = lax.psum_scatter(combined.astype(bf16), "shard", scatter_dimension=0, tiled=True)
    grad_second_here = jnp.einsum("etf,edf->td", grad_both, w_expert_in, preferred_element_type=f32)
    gate_cols = lax.dynamic_update_slice_in_dim(
        jnp.zeros((grad_gates_here.shape[0], EXPERTS), f32),
        grad_gates_here,
        shard_at * own_experts,
        axis=1,
    )
    gate_high = gate_cols.astype(bf16)
    gate_low = (gate_cols - gate_high.astype(f32)).astype(bf16)
    back_rows = jnp.concatenate(
        [
            grad_second_here.astype(bf16),
            gate_high,
            gate_low,
            jnp.zeros((gate_cols.shape[0], PAD - 2 * EXPERTS), bf16),
        ],
        axis=1,
    )
    back_own = lax.psum_scatter(back_rows, "shard", scatter_dimension=0, tiled=True)
    grad_in_here = jnp.einsum("td,etf->edf", second_all, grad_both, preferred_element_type=f32)
    grad_down_here = jnp.einsum("etf,td->efd", gated, dy_all, preferred_element_type=f32)
    grad_in_own = lax.psum(grad_in_here.astype(bf16), "rep").astype(f32)
    grad_down_own = lax.psum(grad_down_here.astype(bf16), "rep").astype(f32)
    mixed = (middle + combined_own.astype(f32)).astype(bf16)
    gate_back = back_own[:, model_width : model_width + 2 * EXPERTS].astype(f32)
    grad_gates = gate_back[:, :EXPERTS] + gate_back[:, EXPERTS:]
    grad_logits = (
        gates_own * (grad_gates - jnp.sum(gates_own * grad_gates, axis=1, keepdims=True))
    ).astype(bf16)
    grad_router = jnp.einsum("td,te->de", second_low, grad_logits, preferred_element_type=f32)
    grad_second = back_own[:, :model_width].astype(f32) + jnp.einsum(
        "te,de->td", grad_logits, router_full, preferred_element_type=f32
    )
    grad_mid_norm, grad_gain_mid = norm_back(grad_second, normed_mid, scale_mid, gain_mid)
    grad_middle = grad_final + grad_mid_norm
    grad_branch = grad_middle.astype(bf16)
    grad_out_w = jnp.einsum("ta,td->ad", att_low, grad_branch, preferred_element_type=f32)
    grad_att = jnp.einsum("td,ad->ta", grad_branch, out_w, preferred_element_type=f32).astype(bf16)
    grad_query_rot, grad_key_rot, grad_value_rows = attend_back(
        query_rows,
        key_rows,
        value_rows,
        doc_ids,
        log_sums,
        grad_att.reshape(row_count, KV_HEADS, groups, HEAD_DIM),
    )
    grad_query_pre = (
        unrotate(grad_query_rot.reshape(row_count, HEADS, HEAD_DIM), cosine, sine_table)
        .astype(bf16)
        .reshape(row_count, query_cols)
    )
    grad_key_pre = unrotate(grad_key_rot, cosine, sine_table).astype(bf16)
    grad_pre = jnp.concatenate(
        [
            grad_query_pre,
            grad_key_pre.reshape(row_count, kv_cols),
            grad_value_rows.astype(bf16).reshape(row_count, kv_cols),
        ],
        axis=1,
    )
    grad_qkv = jnp.einsum("td,tc->dc", first_low, grad_pre, preferred_element_type=f32)
    columns = jnp.einsum("tc,dc->td", grad_pre, qkv_w, preferred_element_type=f32)
    grad_in_norm, grad_gain_in = norm_back(columns, normed_in, scale_in, gain_in)
    grad_tokens = grad_middle + grad_in_norm
    joint = jnp.concatenate(
        [
            grad_qkv.astype(bf16),
            grad_out_w.astype(bf16),
            grad_router.astype(bf16),
            grad_gain_in.astype(bf16)[:, None],
            grad_gain_mid.astype(bf16)[:, None],
            jnp.zeros((model_width, PAD - EXPERTS - 2), bf16),
        ],
        axis=1,
    )
    joint_own = reduce_joint(joint).astype(f32)
    edges = [0]
    for width in (query_cols, kv_cols, kv_cols, w_out.shape[1], EXPERTS, 1, 1):
        edges.append(edges[-1] + width)
    pieces = [joint_own[:, a:b] for a, b in zip(edges[:-1], edges[1:])]
    query_own, key_own, value_own, out_own, router_own, gain_in_own, gain_mid_own = pieces
    return (
        mixed,
        grad_tokens,
        gain_in_own[:, 0],
        query_own,
        key_own,
        value_own,
        out_own,
        gain_mid_own[:, 0],
        router_own,
        grad_in_own,
        grad_down_own,
    )


def reduce_joint(joint):
    part = lax.psum_scatter(joint, "shard", scatter_dimension=0, tiled=True)
    return lax.psum(part, "rep")


def experts(rows, dy_rows, gates, in_w, down_w):
    f32, bf16 = (jnp.float32, jnp.bfloat16)
    both = jnp.einsum("td,edf->etf", rows, in_w, preferred_element_type=f32)
    half_width = both.shape[-1] // 2
    gate_part, up_part = (both[..., :half_width], both[..., half_width:])
    sigmoid_gate = jax.nn.sigmoid(gate_part)
    silu_gate = gate_part * sigmoid_gate
    hidden = (silu_gate * up_part).astype(bf16).astype(f32)
    back = jnp.einsum("td,efd->etf", dy_rows, down_w, preferred_element_type=f32)
    gate_cols = gates.T[:, :, None]
    grad_gates = jnp.sum(hidden * back, axis=-1).T
    gated = (hidden * gate_cols).astype(bf16)
    grad_hidden = back * gate_cols
    grad_gate = grad_hidden * up_part * sigmoid_gate * (1.0 + gate_part * (1.0 - sigmoid_gate))
    grad_both = jnp.concatenate([grad_gate, grad_hidden * silu_gate], axis=-1).astype(bf16)
    return (gated, grad_both, grad_gates)


def solution(mesh):
    in_specs = (
        P(("rep", "shard"), None),
        P(("rep", "shard")),
        P(("rep", "shard"), None),
        P("shard"),
        P("shard", None),
        P("shard", None),
        P("shard", None),
        P("shard", None),
        P("shard"),
        P("shard", None),
        P("shard", None, None),
        P("shard", None, None),
        P(("rep", "shard"), None),
    )
    out_specs = (
        P(("rep", "shard"), None),
        P(("rep", "shard"), None),
        P("shard"),
        P("shard", None),
        P("shard", None),
        P("shard", None),
        P("shard", None),
        P("shard"),
        P("shard", None),
        P("shard", None, None),
        P("shard", None, None),
    )
    return jax.shard_map(shards, mesh=mesh, in_specs=in_specs, out_specs=out_specs, check_vma=False)
```

profile of v0, /device:TPU:0, one launch (start us, length us, event | category | flops | bytes accessed | tf_op | source)
XLA Modules:
  0.0 990.5 jit_solution(4883131591927317545)
XLA Ops:
  7.2 0.8 broadcast_in_dim.44
  8.8 0.8 copy.129
  9.7 3.1 concatenate.49
  14.4 1.3 maximum_maximum_fusion.1
  15.8 1.5 copy.128
  18.9 81.9 %all-gather.5.cloned.1.call-done = bf16[1024,2176]{1,0:T(8,128)(2,1)} async-done(((bf16[256,2176]{1,0:T(8,128)(2,1)}), bf16[1024,2176]{1,0:T(8,128)(2,1)}) %all-gather.5.cloned.1.call-update) | async-done | bytes 4456464 | tf_op jit(solution)/shard_map/all_gather | solution.py:118
  100.8 1.5 convert_reduce_fusion
  102.3 4.8 fusion.24
  107.1 1.6 slice.186
  108.6 1.1 slice.183
  109.7 0.9 slice.274
  110.6 1.9 copy.134
  112.5 2.5 copy.133
  115.0 2.0 copy.132
  117.1 1.4 subtract_convert_fusion.3
  118.9 7.7 fusion.70
  126.6 8.3 fusion.6
  135.6 8.7 fusion.41
  144.2 2.6 all-gather.7.cloned.1.call-done
  146.8 3.3 multiply_reduce_fusion.2
  150.1 1.2 multiply_convert_fusion.3
  151.5 85.6 %all-gather.11.cloned.1.call-done = bf16[2048,1152]{0,1:T(8,128)(2,1)} async-done(((bf16[512,1152]{0,1:T(8,128)(2,1)}), bf16[2048,1152]{0,1:T(8,128)(2,1)}) %all-gather.11.cloned.1.call-update) | async-done | bytes 4718608 | tf_op jit(solution)/shard_map/all_gather | solution.py:118
  237.1 81.2 %all-gather.9.cloned.1.call-done = bf16[2048,1024]{0,1:T(8,128)(2,1)} async-done(((bf16[512,1024]{0,1:T(8,128)(2,1)}), bf16[2048,1024]{0,1:T(8,128)(2,1)}) %all-gather.9.cloned.1.call-update) | async-done | bytes 4194320 | tf_op jit(solution)/shard_map/all_gather | solution.py:118
  318.3 3.1 fusion.71
  321.5 0.9 fusion.59
  322.4 0.9 fusion.58
  323.3 23.1 %convolution_bitcast_fusion = f32[4,2048,1024]{1,2,0:T(8,128)} fusion(bf16[4,1024,1024]{2,1,0:T(8,128)(2,1)} %param.31, bf16[2048,1024]{0,1:T(8,128)(2,1)S(1)} %copy-done.9), kind=kOutput, calls=%fused_computation.2 | convolution fusion | flops 17179869184 | bytes 46137344 | tf_op jit(solution)/shard_map/td,edf->etf/dot_general | solution.py:307
  346.4 28.4 %multiply_convert_fusion.1 = (bf16[4,2048,512]{1,2,0:T(8,128)(2,1)}, bf16[4,2048,512]{1,2,0:T(8,128)(2,1)}, f32[4,2048]{1,0:T(4,128)S(1)}, bf16[4,2048,512]{1,2,0:T(8,128)(2,1)}) fusion(f32[4,2048,1024]{1,2,0:T(8,128)} %convolution_bitcast_fusion, f32[4,2048]{1,0:T(4,128)S(1)} %dynamic-slice_bitcast_fusion, bf16[4,512,1024]{2,1,0:T(8,128)(2,1)} %param.32, ...), kind=kOutput, calls=%fused_computation.15 | convolution fusion | flops 8669618176 | bytes 67174400 | tf_op jit(solution)/shard_map/td,efd->etf/dot_general | solution.py:313
  374.8 22.7 %bitcast_convert_fusion = bf16[2048,1024]{0,1:T(8,128)(2,1)S(1)} fusion(bf16[4,1024,1024]{2,1,0:T(8,128)(2,1)} %param.31, bf16[4,2048,512]{1,2,0:T(8,128)(2,1)} %get-tuple-element.122, bf16[4,2048,512]{1,2,0:T(8,128)(2,1)} %get-tuple-element.121), kind=kOutput, calls=%fused_computation.26 | convolution fusion | flops 17215520768 | bytes 29360128 | tf_op jit(solution)/shard_map/etf,edf->td/dot_general | solution.py:204
  397.6 6.7 maximum_maximum_fusion
  404.4 14.1 %bitcast_convert_fusion.1 = bf16[2048,1024]{0,1:T(8,128)(2,1)} fusion(bf16[4,512,1024]{2,1,0:T(8,128)(2,1)} %param.32, bf16[4,2048,512]{1,2,0:T(8,128)(2,1)} %get-tuple-element.124, f32[4,2048]{1,0:T(4,128)S(1)} %dynamic-slice_bitcast_fusion), kind=kOutput, calls=%fused_computation.27 | convolution fusion | flops 8604614656 | bytes 16809984 | tf_op jit(solution)/shard_map/etf,efd->td/dot_general | solution.py:202
  419.9 68.4 %reduce-scatter.6.cloned.1.call-done = bf16[512,1152]{0,1:T(8,128)(2,1)} async-done(((bf16[2048,1152]{0,1:T(8,128)(2,1)}), bf16[512,1152]{0,1:T(8,128)(2,1)}) %reduce-scatter.6.cloned.1.call-update) | async-done | bytes 1179664 | tf_op jit(solution)/shard_map/reduce_scatter | solution.py:222
  489.1 3.3 multiply_reduce_fusion
  492.4 75.3 %reduce-scatter.4.cloned.1.call-done = bf16[512,1024]{0,1:T(8,128)(2,1)} async-done(((bf16[2048,1024]{0,1:T(8,128)(2,1)}), bf16[512,1024]{0,1:T(8,128)(2,1)}) %reduce-scatter.4.cloned.1.call-update) | async-done | bytes 1048592 | tf_op jit(solution)/shard_map/reduce_scatter | solution.py:203
  567.7 3.6 multiply_add_fusion
  571.4 1.3 copy-done.8
  572.7 1.3 convolution_convert_fusion.2
  574.8 15.1 %fusion.2 = (f32[8,2,512]{2,1,0:T(2,128)S(1)}, f32[8,512,512,2]{2,1,3,0:T(8,128)}) fusion(f32[8,2,512,512]{2,3,1,0:T(8,128)} %get-tuple-element.142, f32[8,2,512]{2,1,0:T(2,128)} %bitcast.136, bf16[512,8,64,1]{0,2,3,1:T(8,128)(2,1)S(1)} %bitcast.125, bf16[512,8,2,64]{0,3,2,1:T(8,128)(2,1)S(1)} %bitcast.119), kind=kOutput, calls=%fused_computation.8 | convolution fusion | flops 549445632 | bytes 35192832 | tf_op jit(solution)/shard_map/qgrd,kgd->grqk/dot_general | solution.py:93
  589.9 1.3 slice-done.3
  591.2 8.3 fusion.4
  599.6 3.4 copy-done
  603.0 2.8 convolution_multiply_fusion
  605.8 6.0 fusion.46
  611.8 3.6 fusion.47
  615.5 4.7 convolution_convert_fusion.1
  620.2 1.0 convolution_convert_fusion.3
  622.4 4.4 convolution_convert_fusion
  626.9 5.0 fusion.39
  632.1 0.8 copy.153
  633.0 0.9 convert_element_type.231
  634.6 10.6 %concatenate.62 = bf16[1024,3200]{1,0:T(8,128)(2,1)} concatenate(bf16[1024,2048]{1,0:T(8,128)(2,1)} %convolution_convert_fusion, bf16[1024,1024]{1,0:T(8,128)(2,1)S(1)} %copy-done.17, bf16[1024,16]{1,0:T(8,128)(2,1)} %copy.153, bf16[1024,1]{1,0:T(8,128)(2,1)S(1)} %convert_element_type.230, bf16[1024,1]{1,0:T(8,128)(2,1)} %convert_element_type.231, bf16[1024,110]{1,0:T(8,128)(2,1)} %broadcast_in_dim.43), dimensions={1} | concatenate | bytes 13107200 | tf_op jit(solution)/shard_map/concatenate | solution.py:268
  646.0 13.8 %fusion.31 = bf16[4,512,1024]{2,1,0:T(8,128)(2,1)} fusion(bf16[2048,1152]{0,1:T(8,128)(2,1)} %all-gather.11.cloned.1.call-done, bf16[4,2048,512]{1,2,0:T(8,128)(2,1)} %get-tuple-element.124, f32[4,2048]{1,0:T(4,128)S(1)} %copy-done.36), kind=kOutput, calls=%fused_computation.50 | convolution fusion | flops 8604614656 | bytes 16809984 | tf_op jit(solution)/shard_map/etf,td->efd/dot_general | solution.py:224
  659.8 24.8 %convert_bitcast_fusion = bf16[4,1024,1024]{1,2,0:T(8,128)(2,1)} fusion(bf16[4,2048,512]{1,2,0:T(8,128)(2,1)} %get-tuple-element.122, bf16[4,2048,512]{1,2,0:T(8,128)(2,1)} %get-tuple-element.121, bf16[2048,1024]{0,1:T(8,128)(2,1)} %all-gather.9.cloned.1.call-done), kind=kOutput, calls=%fused_computation.28 | convolution fusion | flops 17217617920 | bytes 29360128 | tf_op jit(solution)/shard_map/td,etf->edf/dot_general | solution.py:223
  684.6 76.3 %reduce-scatter.8.cloned.1.call-done = bf16[256,3200]{1,0:T(8,128)(2,1)} async-done(((bf16[1024,3200]{1,0:T(8,128)(2,1)}), bf16[256,3200]{1,0:T(8,128)(2,1)}) %reduce-scatter.8.cloned.1.call-update) | async-done | bytes 1638416 | tf_op jit(solution)/shard_map/reduce_scatter | solution.py:301
  761.0 2.7 fusion.38
  763.7 1.8 copy.159
  765.5 1.3 copy.158
  766.8 191.1 %all-reduce.3.cloned.1.call-done = (bf16[4,1024,1024]{1,2,0:T(8,128)(2,1)}, bf16[256,3200]{1,0:T(8,128)(2,1)}, bf16[4,512,1024]{2,1,0:T(8,128)(2,1)}) async-done(((bf16[4,1024,1024]{1,2,0:T(8,128)(2,1)}, bf16[256,3200]{1,0:T(8,128)(2,1)}, bf16[4,512,1024]{2,1,0:T(8,128)(2,1)}), (bf16[4,1024,1024]{1,2,0:T(8,128)(2,1)}, bf16[256,3200]{1,0:T(8,128)(2,1)}, ...) | async-done | bytes 14221328 | tf_op jit(solution)/shard_map/psum | solution.py:225
  957.9 1.8 convert_element_type.222
  959.9 1.6 fusion.68
  961.4 1.1 fusion.69
  962.6 12.5 %copy.161 = f32[4,1024,1024]{2,1,0:T(8,128)} copy(bf16[4,1024,1024]{1,2,0:T(8,128)(2,1)} %get-tuple-element.114) | data formatting | bytes 25165824
  975.1 6.6 convert_element_type.227
  981.7 0.8 slice_reduce_fusion
  (155 shorter events, 11.9 us)
Async XLA Ops:
  7.2 6.5 copy-start.22
  7.2 7.0 copy-start.39
  7.2 93.6 %all-gather.5.cloned.1.call-start = ((), (), s32[]{:S(2)}) async-start(), calls=%async_computation.3 | async-start | bytes 5570560 | tf_op jit(solution)/shard_map/all_gather | solution.py:118
  12.8 4.4 copy-start.34
  12.8 134.0 %all-gather.7.cloned.1.call-start = ((), (), s32[]{:S(2)}) async-start(), calls=%async_computation.4 | async-start | bytes 2621440 | tf_op jit(solution)/shard_map/all_gather | solution.py:118
  13.6 223.5 %all-gather.11.cloned.1.call-start = ((), (), s32[]{:S(2)}) async-start(), calls=%async_computation.6 | async-start | bytes 5898240 | tf_op jit(solution)/shard_map/all_gather | solution.py:118
  14.2 92.8 %copy-start.5 = (bf16[512,1024]{0,1:T(8,128)(2,1)}, bf16[512,1024]{0,1:T(8,128)(2,1)S(1)}, u32[]{:S(2)}) copy-start(bf16[512,1024]{0,1:T(8,128)(2,1)S(1)} %copy.139) | copy-start | bytes 3145732
  15.7 302.6 %all-gather.9.cloned.1.call-start = ((), (), s32[]{:S(2)}) async-start(), calls=%async_computation.5 | async-start | bytes 5242880 | tf_op jit(solution)/shard_map/all_gather | solution.py:118
  17.3 129.5 %copy-start.3 = (bf16[512,1024]{0,1:T(8,128)(2,1)}, bf16[512,1024]{0,1:T(8,128)(2,1)S(1)}, u32[]{:S(2)}) copy-start(bf16[512,1024]{0,1:T(8,128)(2,1)S(1)} %copy.128) | copy-start | bytes 3145732
  18.3 88.8 %copy-start.40 = (f32[512]{0:T(512)}, f32[512]{0:T(512)S(1)}, u32[]{:S(2)}) copy-start(f32[512]{0:T(512)S(1)} %add_rsqrt_fusion.1) | copy-start | bytes 6148
  18.7 99.8 %copy-start.18 = (f32[512,32]{0,1:T(8,128)}, f32[512,32]{0,1:T(8,128)S(1)}, u32[]{:S(2)}) copy-start(f32[512,32]{0,1:T(8,128)S(1)} %get-tuple-element.139) | copy-start | bytes 196612
  18.7 99.8 %copy-start.20 = (f32[512,32]{0,1:T(8,128)}, f32[512,32]{0,1:T(8,128)S(1)}, u32[]{:S(2)}) copy-start(f32[512,32]{0,1:T(8,128)S(1)} %get-tuple-element.140) | copy-start | bytes 196612
  102.3 4.8 copy-start.37
  118.5 8.1 copy-start.23
  118.5 8.1 copy-start.25
  118.8 7.7 copy-start.13
  118.9 7.7 copy-start.15
  126.6 8.4 copy-start.29
  126.6 9.0 copy-start.11
  135.0 0.6 copy-start.31
  151.3 336.9 %reduce-scatter.6.cloned.1.call-start = ((), (), s32[]{:S(2)}) async-start(), calls=%async_computation.8 | async-start | bytes 5898240 | tf_op jit(solution)/shard_map/reduce_scatter | solution.py:222
  318.3 4.9 copy-start.9
  323.3 81.1 %copy-start.35 = (f32[4,2048]{1,0:T(4,128)}, f32[4,2048]{1,0:T(4,128)S(1)}, u32[]{:S(2)}) copy-start(f32[4,2048]{1,0:T(4,128)S(1)} %dynamic-slice_bitcast_fusion) | copy-start | bytes 98308
  404.3 163.4 %reduce-scatter.4.cloned.1.call-start = ((), (), s32[]{:S(2)}) async-start(), calls=%async_computation.7 | async-start | bytes 5242880 | tf_op jit(solution)/shard_map/reduce_scatter | solution.py:203
  418.4 0.8 copy-start.30
  418.4 0.8 copy-start.32
  418.5 149.3 %copy-start.6 = (bf16[512,1024]{0,1:T(8,128)(2,1)S(1)}, bf16[512,1024]{0,1:T(8,128)(2,1)}, u32[]{:S(2)}) copy-start(bf16[512,1024]{0,1:T(8,128)(2,1)} %copy-done.5) | copy-start | bytes 3145732
  418.5 342.5 %reduce-scatter.8.cloned.1.call-start = ((), (), s32[]{:S(2)}) async-start(), calls=%async_computation.9 | async-start | bytes 8192000 | tf_op jit(solution)/shard_map/reduce_scatter | solution.py:301
  567.7 5.0 copy-start.42
  571.4 1.3 copy-start.8
  572.7 2.1 copy-start.12
  574.7 15.1 %slice-start = ((s8[16777216]{0:T(1024)(128)(4,1)}), s8[4194304]{0:T(1024)(128)(4,1)S(1)}, s32[]{:S(2)}) async-start(s8[16777216]{0:T(1024)(128)(4,1)} %bitcast.117), calls=%async_computation.11 | async-start | bytes 8388608
  574.8 15.1 %slice-start.1 = ((s8[16777216]{0:T(1024)(128)(4,1)}), s8[4194304]{0:T(1024)(128)(4,1)S(1)}, s32[]{:S(2)}) async-start(s8[16777216]{0:T(1024)(128)(4,1)} %bitcast.117), calls=%async_computation.12 | async-start | bytes 8388608
  574.8 15.1 %slice-start.2 = ((s8[16777216]{0:T(1024)(128)(4,1)}), s8[4194304]{0:T(1024)(128)(4,1)S(1)}, s32[]{:S(2)}) async-start(s8[16777216]{0:T(1024)(128)(4,1)} %bitcast.117), calls=%async_computation.13 | async-start | bytes 8388608
  574.8 16.4 %slice-start.3 = ((s8[16777216]{0:T(1024)(128)(4,1)}), s8[4194304]{0:T(1024)(128)(4,1)S(1)}, s32[]{:S(2)}) async-start(s8[16777216]{0:T(1024)(128)(4,1)} %bitcast.117), calls=%async_computation.14 | async-start | bytes 8388608
  574.8 16.4 %copy-start.28 = (f32[2,8,512]{2,1,0:T(8,128)S(1)}, f32[2,8,512]{2,1,0:T(8,128)}, u32[]{:S(2)}) copy-start(f32[2,8,512]{2,1,0:T(8,128)} %log_add_fusion) | copy-start | bytes 98308
  591.2 11.7 %copy-start.24 = (bf16[512,8,32]{0,2,1:T(8,128)(2,1)S(1)}, bf16[512,8,32]{0,2,1:T(8,128)(2,1)}, u32[]{:S(2)}) copy-start(bf16[512,8,32]{0,2,1:T(8,128)(2,1)} %copy-done.23) | copy-start | bytes 786436
  591.2 11.7 %copy-start.26 = (bf16[512,8,32]{0,2,1:T(8,128)(2,1)S(1)}, bf16[512,8,32]{0,2,1:T(8,128)(2,1)}, u32[]{:S(2)}) copy-start(bf16[512,8,32]{0,2,1:T(8,128)(2,1)} %copy-done.25) | copy-start | bytes 786436
  599.6 3.4 copy-start
  603.0 2.9 copy-start.14
  603.0 2.9 copy-start.16
  615.4 6.5 copy-start.27
  615.4 4.8 copy-start.2
  615.4 5.8 copy-start.7
  615.4 5.8 copy-start.19
  615.4 5.8 copy-start.21
  621.2 1.2 copy-start.4
  621.2 1.2 copy-start.38
  621.2 1.2 copy-start.41
  621.2 5.6 slice-start.4
  622.4 4.4 slice-start.5
  626.9 5.2 copy-start.33
  626.9 7.7 copy-start.17
  645.2 0.8 copy-start.36
  645.3 312.7 %all-reduce.3.cloned.1.call-start = ((), (), s32[]{:S(2)}) async-start(), calls=%async_computation.10 | async-start | bytes 28442624 | tf_op jit(solution)/shard_map/psum | solution.py:225
  763.7 1.8 copy-start.10
  957.9 1.9 copy-start.1
Sparse Core Ops, SparseCore 0:
  12.9 87.7 all-gather.4
  102.3 44.4 all-gather.6
  149.0 88.1 all-gather.10
  239.1 79.1 all-gather.8
  404.4 83.7 reduce-scatter.5
  490.4 77.2 reduce-scatter.3
  645.4 115.4 reduce-scatter.7
  766.1 191.8 all-reduce.2
where the time goes:
time: 1000 us; the launch traced here: 990 us
  waiting for transfers between devices  663 us (66%)
  matrix products  202 us (20%)
  local copies, waits for them, and re-layouts  60.7 us (6%)
  other arithmetic  49.2 us (5%)
  between operations  15.4 us (2%)
    all_gather x4, waiting for transfers between devices, gather_shard(): return lax.all_gather(piece, 'shard', axis=0, tiled=True)  251 us
    psum x1, waiting for transfers between devices, shards(): grad_in_own = lax.psum(grad_in_here.astype(bf16), 'rep').astype(f32)  191 us
    reduce_scatter x1, waiting for transfers between devices, reduce_joint(): part = lax.psum_scatter(joint, 'shard', scatter_dimension=0, tiled=True)  76.3 us
    reduce_scatter x1, waiting for transfers between devices, shards(): lax.psum_scatter(combined.astype(bf16), 'shard', scatter_dimension=0, til...  75.3 us
    reduce_scatter x1, waiting for transfers between devices, shards(): lax.psum_scatter(back_rows, 'shard', scatter_dimension=0, tiled=True)  68.4 us
    dot_general x1, matrix products, experts(): jnp.einsum('td,efd->etf', dy_rows, down_w, preferred_element_type=f32)  28.4 us
    unnamed x105, local copies, waits for them, and re-layouts  28 us
    dot_general x1, matrix products, shards(): jnp.einsum('td,etf->edf', second_all, grad_both, preferred_element_type=f32)  24.8 us
  transfers between devices with their start and end apart: 8, of which 8 were waited for; matrix products, arithmetic and copies ran while one was open for 12% of the time, Pallas kernels for 0%

commit v1 on v0

--- a/solution.py
+++ b/solution.py
@@ -115,7 +115,39 @@
 
 
 def gather_shard(piece):
-    return lax.all_gather(piece, "shard", axis=0, tiled=True)
+
+    def set_the_regions(mine, named_axis):
+        new, long_array, reply = (
+            lax.axis_size(named_axis),
+            lax.axis_index(named_axis),
+            mine.shape[0],
+        )
+        chunks = []
+        for at, hop_no in enumerate(mine.shape):
+            chunks.append(hop_no * new if at == 0 else hop_no)
+        val2 = mat_out = mine
+        found_now = lax.dynamic_update_slice_in_dim(
+            jnp.zeros(chunks, mine.dtype), mine, long_array * reply, axis=0
+        )
+        for q in range(1, new // 2 + 1):
+            tray = []
+            for at in range(new):
+                tray.append((at, (at + 1) % new))
+            val2 = lax.ppermute(val2, axis_name=named_axis, perm=tray)
+            found_now = lax.dynamic_update_slice_in_dim(
+                found_now, val2, (long_array - q) % new * reply, axis=0
+            )
+            if 2 * q < new:
+                pieces_in = []
+                for at in range(new):
+                    pieces_in.append((at, (at - 1) % new))
+                mat_out = lax.ppermute(mat_out, axis_name=named_axis, perm=pieces_in)
+                found_now = lax.dynamic_update_slice_in_dim(
+                    found_now, mat_out, (long_array + q) % new * reply, axis=0
+                )
+        return found_now
+
+    return set_the_regions(piece, "shard")
 
 
 def shards(

time: 1000 us -> 1000 us (level)
  waiting for transfers between devices: 663 us -> 576 us
  starting transfers between devices: 0.33 us -> 51.3 us
  local copies, waits for them, and re-layouts: 60.7 us -> 98.5 us
    all_gather x4 -> x0, waiting for transfers between devices: 251 us -> none  [gather_shard(): return lax.all_gather(piece, 'shard', axis=0, tiled=True)]
    ppermute x0 -> x12, waiting for transfers between devices: none -> 166 us  [the longest x8 147 us: set_the_regions(): val2 = lax.ppermute(val2, axis_name=named_axis, perm=tray)]
    ppermute x0 -> x12, starting transfers between devices: none -> 51.1 us  [the longest x8 37.6 us: set_the_regions(): val2 = lax.ppermute(val2, axis_name=named_axis, perm=tray)]
    dynamic_update_slice x0 -> x15, local copies, waits for them, and re-layouts: none -> 19.1 us  [the longest x8 10.6 us: set_the_regions(): lax.dynamic_update_slice_in_dim(found_now, val2, (long_array - q) % new *...]
    unnamed x105 -> x113, local copies, waits for them, and re-layouts: 28 us -> 29.9 us
  transfers between devices with their start and end apart: 8 -> 16, of which waited for: 8 -> 12; matrix products, arithmetic and copies ran while one was open for 12% -> 15% of each run, Pallas kernels for 0% -> 0%
where the time goes in v1:
time: 1000 us; the launch traced here: 994 us
  waiting for transfers between devices  576 us (58%)
  matrix products  203 us (20%)
  local copies, waits for them, and re-layouts  98.5 us (10%)
  starting transfers between devices  51.3 us (5%)
  other arithmetic  51.1 us (5%)
  between operations  14.9 us (1%)
    psum x1, waiting for transfers between devices, shards(): grad_in_own = lax.psum(grad_in_here.astype(bf16), 'rep').astype(f32)  191 us
    ppermute x8, waiting for transfers between devices, set_the_regions(): val2 = lax.ppermute(val2, axis_name=named_axis, perm=tray)  147 us
    reduce_scatter x1, waiting for transfers between devices, reduce_joint(): part = lax.psum_scatter(joint, 'shard', scatter_dimension=0, tiled=True)  76.5 us
    reduce_scatter x1, waiting for transfers between devices, shards(): lax.psum_scatter(combined.astype(bf16), 'shard', scatter_dimension=0, til...  74.4 us
    reduce_scatter x1, waiting for transfers between devices, shards(): lax.psum_scatter(back_rows, 'shard', scatter_dimension=0, tiled=True)  67.9 us
    ppermute x8, starting transfers between devices, set_the_regions(): val2 = lax.ppermute(val2, axis_name=named_axis, perm=tray)  37.6 us
    unnamed x113, local copies, waits for them, and re-layouts  29.9 us
    dot_general x1, matrix products, experts(): jnp.einsum('td,efd->etf', dy_rows, down_w, preferred_element_type=f32)  28.3 us
  transfers between devices with their start and end apart: 16, of which 12 were waited for; matrix products, arithmetic and copies ran while one was open for 15% of the time, Pallas kernels for 0%

profile of v1, /device:TPU:0, one launch (start us, length us, event | category | flops | bytes accessed | tf_op | source)
XLA Modules:
  0.0 994.5 jit_solution(17348019589677428760)
XLA Ops:
  9.6 2.4 concatenate.49
  12.0 3.1 collective-permute-start
  15.1 2.1 collective-permute-start.1
  17.2 3.8 collective-permute-start.4
  22.7 2.8 broadcast_in_dim.92
  25.5 1.8 maximum_maximum_fusion.1
  29.4 2.0 copy-done.10
  33.7 44.1 %collective-permute-done.3 = bf16[256,1024]{1,0:T(8,128)(2,1)} collective-permute-done((bf16[256,1024]{1,0:T(8,128)(2,1)}, bf16[256,1024]{1,0:T(8,128)(2,1)}, u32[]{:S(2)}, u32[]{:S(2)}) %collective-permute-start.3) | collective-permute-done | bytes 524320 | tf_op jit(solution)/shard_map/ppermute | solution.py:136
  77.8 9.8 collective-permute-start.5
  90.9 3.4 collective-permute-start.2
  94.3 1.9 constant_dynamic-update-slice_fusion.10
  96.2 1.9 constant_dynamic-update-slice_fusion.9
  98.1 27.4 %collective-permute-done.5 = bf16[256,1024]{1,0:T(8,128)(2,1)S(1)} collective-permute-done((bf16[256,1024]{1,0:T(8,128)(2,1)}, bf16[256,1024]{1,0:T(8,128)(2,1)S(1)}, u32[]{:S(2)}, u32[]{:S(2)}) %collective-permute-start.5) | collective-permute-done | bytes 524320 | tf_op jit(solution)/shard_map/ppermute | solution.py:136
  128.0 1.7 copy.146
  131.9 16.7 %collective-permute-done.2 = bf16[256,2176]{1,0:T(8,128)(2,1)} collective-permute-done((bf16[256,2176]{1,0:T(8,128)(2,1)}, bf16[256,2176]{1,0:T(8,128)(2,1)}, u32[]{:S(2)}, u32[]{:S(2)}) %collective-permute-start.2) | collective-permute-done | bytes 1114144 | tf_op jit(solution)/shard_map/ppermute | solution.py:136
  152.2 4.8 fusion.24
  160.5 1.9 copy.150
  162.4 2.5 copy.149
  169.1 9.1 fusion.70
  178.2 8.3 fusion.6
  186.5 7.6 fusion.41
  194.1 3.3 multiply_reduce_fusion.2
  199.1 3.8 collective-permute-start.10
  202.9 3.8 collective-permute-start.7
  206.8 20.3 %collective-permute-done.6 = bf16[512,1024]{0,1:T(8,128)(2,1)} collective-permute-done((bf16[512,1024]{0,1:T(8,128)(2,1)S(1)}, bf16[512,1024]{0,1:T(8,128)(2,1)}, u32[]{:S(2)}, u32[]{:S(2)}) %collective-permute-start.6) | collective-permute-done | bytes 1048608 | tf_op jit(solution)/shard_map/ppermute | solution.py:136
  227.1 21.3 %collective-permute-start.8 = (bf16[512,1024]{0,1:T(8,128)(2,1)}, bf16[512,1024]{0,1:T(8,128)(2,1)}, u32[]{:S(2)}, u32[]{:S(2)}) collective-permute-start(bf16[512,1024]{0,1:T(8,128)(2,1)} %collective-permute-done.6), channel_id=1, source_target_pairs={{0,1},{1,2},{2,3},{3,0},{4,5},{5,6},{6,7},{7,4},{8,9},{9,10},{10,1... | collective-permute-start | bytes 3145736 | tf_op jit(solution)/shard_map/ppermute | solution.py:136
  248.4 2.4 constant_dynamic-update-slice_fusion.2
  250.8 1.9 collective-permute-done.10
  252.7 2.4 constant_dynamic-update-slice_fusion.1
  255.8 2.6 broadcast_in_dim.49
  259.5 18.1 %collective-permute-done.11 = bf16[512,1152]{0,1:T(8,128)(2,1)S(1)} collective-permute-done((bf16[512,1152]{0,1:T(8,128)(2,1)}, bf16[512,1152]{0,1:T(8,128)(2,1)S(1)}, u32[]{:S(2)}, u32[]{:S(2)}) %collective-permute-start.11) | collective-permute-done | bytes 1179680 | tf_op jit(solution)/shard_map/ppermute | solution.py:136
  280.2 16.7 %collective-permute-done.7 = bf16[512,1024]{0,1:T(8,128)(2,1)} collective-permute-done((bf16[512,1024]{0,1:T(8,128)(2,1)S(1)}, bf16[512,1024]{0,1:T(8,128)(2,1)}, u32[]{:S(2)}, u32[]{:S(2)}) %collective-permute-start.7) | collective-permute-done | bytes 1048608 | tf_op jit(solution)/shard_map/ppermute | solution.py:144
  300.5 20.4 %collective-permute-done.8 = bf16[512,1024]{0,1:T(8,128)(2,1)} collective-permute-done((bf16[512,1024]{0,1:T(8,128)(2,1)}, bf16[512,1024]{0,1:T(8,128)(2,1)}, u32[]{:S(2)}, u32[]{:S(2)}) %collective-permute-start.8) | collective-permute-done | bytes 1048608 | tf_op jit(solution)/shard_map/ppermute | solution.py:136
  323.5 25.2 %convolution_bitcast_fusion = f32[4,2048,1024]{1,2,0:T(8,128)} fusion(bf16[4,1024,1024]{2,1,0:T(8,128)(2,1)} %param.31, bf16[2048,1024]{1,0:T(8,128)(2,1)} %constant_dynamic-update-slice_fusion.4), kind=kOutput, calls=%fused_computation.2 | convolution fusion | flops 17179869184 | bytes 46137344 | tf_op jit(solution)/shard_map/td,edf->etf/dot_general | solution.py:339
  348.7 3.4 fusion.71
  353.9 28.3 %multiply_convert_fusion.1 = (bf16[4,2048,512]{1,2,0:T(8,128)(2,1)}, bf16[4,2048,512]{1,2,0:T(8,128)(2,1)}, f32[4,2048]{1,0:T(4,128)S(1)}, bf16[4,2048,512]{1,2,0:T(8,128)(2,1)}) fusion(f32[4,2048,1024]{1,2,0:T(8,128)} %convolution_bitcast_fusion, f32[4,2048]{1,0:T(4,128)S(1)} %dynamic-slice_bitcast_fusion, bf16[4,512,1024]{2,1,0:T(8,128)(2,1)} %param.32, ...), kind=kOutput, calls=%fused_computation.15 | convolution fusion | flops 8669618176 | bytes 67174400 | tf_op jit(solution)/shard_map/td,efd->etf/dot_general | solution.py:345
  382.3 23.1 %bitcast_convert_fusion = bf16[2048,1024]{0,1:T(8,128)(2,1)S(1)} fusion(bf16[4,1024,1024]{2,1,0:T(8,128)(2,1)} %param.31, bf16[4,2048,512]{1,2,0:T(8,128)(2,1)} %get-tuple-element.120, bf16[4,2048,512]{1,2,0:T(8,128)(2,1)} %get-tuple-element.119), kind=kOutput, calls=%fused_computation.26 | convolution fusion | flops 17215520768 | bytes 29360128 | tf_op jit(solution)/shard_map/etf,edf->td/dot_general | solution.py:236
  405.5 6.3 maximum_maximum_fusion
  411.9 14.0 %bitcast_convert_fusion.1 = bf16[2048,1024]{0,1:T(8,128)(2,1)} fusion(bf16[4,512,1024]{2,1,0:T(8,128)(2,1)} %param.32, bf16[4,2048,512]{1,2,0:T(8,128)(2,1)} %get-tuple-element.122, f32[4,2048]{1,0:T(4,128)S(1)} %dynamic-slice_bitcast_fusion), kind=kOutput, calls=%fused_computation.27 | convolution fusion | flops 8604614656 | bytes 16809984 | tf_op jit(solution)/shard_map/etf,efd->td/dot_general | solution.py:234
  427.3 67.9 %reduce-scatter.6.cloned.1.call-done = bf16[512,1152]{0,1:T(8,128)(2,1)} async-done(((bf16[2048,1152]{0,1:T(8,128)(2,1)}), bf16[512,1152]{0,1:T(8,128)(2,1)}) %reduce-scatter.6.cloned.1.call-update) | async-done | bytes 1179664 | tf_op jit(solution)/shard_map/reduce_scatter | solution.py:254
  496.0 3.3 multiply_reduce_fusion
  500.4 74.4 %reduce-scatter.4.cloned.1.call-done = bf16[512,1024]{0,1:T(8,128)(2,1)} async-done(((bf16[2048,1024]{0,1:T(8,128)(2,1)}), bf16[512,1024]{0,1:T(8,128)(2,1)}) %reduce-scatter.4.cloned.1.call-update) | async-done | bytes 1048592 | tf_op jit(solution)/shard_map/reduce_scatter | solution.py:235
  574.8 3.9 multiply_add_fusion
  578.7 2.6 convolution_convert_fusion.1
  581.3 3.0 convolution_convert_fusion.2
  585.1 15.1 %fusion.2 = (f32[8,2,512]{2,1,0:T(2,128)S(1)}, f32[8,512,512,2]{2,1,3,0:T(8,128)}) fusion(f32[8,2,512,512]{2,3,1,0:T(8,128)} %get-tuple-element.144, f32[8,2,512]{2,1,0:T(2,128)} %bitcast.139, bf16[512,8,64,1]{0,2,3,1:T(8,128)(2,1)S(1)} %bitcast.128, bf16[512,8,2,64]{0,3,2,1:T(8,128)(2,1)S(1)} %bitcast.120), kind=kOutput, calls=%fused_computation.8 | convolution fusion | flops 549445632 | bytes 35192832 | tf_op jit(solution)/shard_map/qgrd,kgd->grqk/dot_general | solution.py:93
  601.6 8.3 fusion.4
  609.9 3.4 copy-done
  613.3 2.9 convolution_multiply_fusion
  616.2 6.0 fusion.46
  622.2 3.5 fusion.47
  625.8 2.0 add_convert_fusion.1
  628.2 4.4 convolution_convert_fusion
  632.6 3.9 fusion.39
  639.3 10.6 %concatenate.62 = bf16[1024,3200]{1,0:T(8,128)(2,1)} concatenate(bf16[1024,2048]{1,0:T(8,128)(2,1)} %convolution_convert_fusion, bf16[1024,1024]{1,0:T(8,128)(2,1)S(1)} %copy-done.16, bf16[1024,16]{1,0:T(8,128)(2,1)S(1)} %copy.172, bf16[1024,1]{1,0:T(8,128)(2,1)} %convert_element_type.230, bf16[1024,1]{1,0:T(8,128)(2,1)} %convert_element_type.231, bf16[1024,110]{1,0:T(8,128)(2,1)} %broadcast_in_dim.97), dimensions={1} | concatenate | bytes 13107200 | tf_op jit(solution)/shard_map/concatenate | solution.py:300
  650.7 13.9 %fusion.31 = bf16[4,512,1024]{2,1,0:T(8,128)(2,1)} fusion(bf16[2048,1152]{0,1:T(8,128)(2,1)} %constant_dynamic-update-slice_fusion, bf16[4,2048,512]{1,2,0:T(8,128)(2,1)} %get-tuple-element.122, f32[4,2048]{1,0:T(4,128)S(1)} %copy-done.37), kind=kOutput, calls=%fused_computation.50 | convolution fusion | flops 8604614656 | bytes 16809984 | tf_op jit(solution)/shard_map/etf,td->efd/dot_general | solution.py:256
  664.6 24.5 %convert_bitcast_fusion = bf16[4,1024,1024]{1,2,0:T(8,128)(2,1)} fusion(bf16[4,2048,512]{1,2,0:T(8,128)(2,1)} %get-tuple-element.120, bf16[4,2048,512]{1,2,0:T(8,128)(2,1)} %get-tuple-element.119, bf16[2048,1024]{1,0:T(8,128)(2,1)} %constant_dynamic-update-slice_fusion.4), kind=kOutput, calls=%fused_computation.28 | convolution fusion | flops 17217617920 | bytes 29360128 | tf_op jit(solution)/shard_map/td,etf->edf/dot_general | solution.py:255
  689.0 76.5 %reduce-scatter.8.cloned.1.call-done = bf16[256,3200]{1,0:T(8,128)(2,1)} async-done(((bf16[1024,3200]{1,0:T(8,128)(2,1)}), bf16[256,3200]{1,0:T(8,128)(2,1)}) %reduce-scatter.8.cloned.1.call-update) | async-done | bytes 1638416 | tf_op jit(solution)/shard_map/reduce_scatter | solution.py:333
  765.6 2.7 fusion.38
  768.3 1.8 copy.177
  771.5 191.0 %all-reduce.3.cloned.1.call-done = (bf16[4,1024,1024]{1,2,0:T(8,128)(2,1)}, bf16[256,3200]{1,0:T(8,128)(2,1)}, bf16[4,512,1024]{2,1,0:T(8,128)(2,1)}) async-done(((bf16[4,1024,1024]{1,2,0:T(8,128)(2,1)}, bf16[256,3200]{1,0:T(8,128)(2,1)}, bf16[4,512,1024]{2,1,0:T(8,128)(2,1)}), (bf16[4,1024,1024]{1,2,0:T(8,128)(2,1)}, bf16[256,3200]{1,0:T(8,128)(2,1)}, ...) | async-done | bytes 14221328 | tf_op jit(solution)/shard_map/psum | solution.py:257
  962.5 1.8 convert_element_type.222
  967.1 12.5 %copy.179 = f32[4,1024,1024]{2,1,0:T(8,128)} copy(bf16[4,1024,1024]{1,2,0:T(8,128)(2,1)} %get-tuple-element.112) | data formatting | bytes 25165824
  979.6 6.6 convert_element_type.227
  (202 shorter events, 56.3 us)
Async XLA Ops:
  7.2 15.3 %copy-start.42 = (s32[512,8]{0,1:T(8,128)S(1)}, s32[512,8]{0,1:T(8,128)}, u32[]{:S(2)}) copy-start(s32[512,8]{0,1:T(8,128)} %param.23) | copy-start | bytes 49156
  7.2 488.0 %reduce-scatter.6.cloned.1.call-start = ((), (), s32[]{:S(2)}) async-start(), calls=%async_computation.4 | async-start | bytes 5898240 | tf_op jit(solution)/shard_map/reduce_scatter | solution.py:254
  12.0 78.9 %collective-permute-start = (bf16[256,2176]{1,0:T(8,128)(2,1)S(1)}, bf16[256,2176]{1,0:T(8,128)(2,1)}, u32[]{:S(2)}, u32[]{:S(2)}) collective-permute-start(bf16[256,2176]{1,0:T(8,128)(2,1)S(1)} %concatenate.49), channel_id=1, source_target_pairs={{0,1},{1,2},{2,3},{3,0},{4,5},{5,6},{6,7},{7,4},{8,9},{9,10},{10,1... | collective-permute-start | bytes 3342344 | tf_op jit(solution)/shard_map/ppermute | solution.py:136
  15.1 112.9 %collective-permute-start.1 = (bf16[256,2176]{1,0:T(8,128)(2,1)S(1)}, bf16[256,2176]{1,0:T(8,128)(2,1)}, u32[]{:S(2)}, u32[]{:S(2)}) collective-permute-start(bf16[256,2176]{1,0:T(8,128)(2,1)S(1)} %concatenate.49), channel_id=1, source_target_pairs={{0,3},{1,0},{2,1},{3,2},{4,7},{5,4},{6,5},{7,6},{8,11},{9,8},{10,9... | collective-permute-start | bytes 3342344 | tf_op jit(solution)/shard_map/ppermute | solution.py:144
  17.2 60.6 %collective-permute-start.3 = (bf16[256,1024]{1,0:T(8,128)(2,1)}, bf16[256,1024]{1,0:T(8,128)(2,1)}, u32[]{:S(2)}, u32[]{:S(2)}) collective-permute-start(bf16[256,1024]{1,0:T(8,128)(2,1)} %param.28), channel_id=1, source_target_pairs={{0,1},{1,2},{2,3},{3,0},{4,5},{5,6},{6,7},{7,4},{8,9},{9,10},{10,1... | collective-permute-start | bytes 1572872 | tf_op jit(solution)/shard_map/ppermute | solution.py:136
  17.2 79.0 %collective-permute-start.4 = (bf16[256,1024]{1,0:T(8,128)(2,1)}, bf16[256,1024]{1,0:T(8,128)(2,1)}, u32[]{:S(2)}, u32[]{:S(2)}) collective-permute-start(bf16[256,1024]{1,0:T(8,128)(2,1)} %param.28), channel_id=1, source_target_pairs={{0,3},{1,0},{2,1},{3,2},{4,7},{5,4},{6,5},{7,6},{8,11},{9,8},{10,9... | collective-permute-start | bytes 1572872 | tf_op jit(solution)/shard_map/ppermute | solution.py:144
  22.5 6.9 copy-start.8
  22.7 5.3 copy-start.35
  27.3 175.7 %collective-permute-start.9 = (bf16[512,1152]{0,1:T(8,128)(2,1)}, bf16[512,1152]{0,1:T(8,128)(2,1)}, u32[]{:S(2)}, u32[]{:S(2)}) collective-permute-start(bf16[512,1152]{0,1:T(8,128)(2,1)} %get-tuple-element.139), channel_id=1, source_target_pairs={{0,1},{1,2},{2,3},{3,0},{4,5},{5,6},{6,7},{7,4},{8,9},{9,10},{10,1... | collective-permute-start | bytes 3538952 | tf_op jit(solution)/shard_map/ppermute | solution.py:136
  29.4 2.1 copy-start.10
  31.5 57.7 %copy-start.26 = (bf16[256,1024]{1,0:T(8,128)(2,1)S(1)}, bf16[256,1024]{1,0:T(8,128)(2,1)}, u32[]{:S(2)}) copy-start(bf16[256,1024]{1,0:T(8,128)(2,1)} %param.28) | copy-start | bytes 1572868
  33.1 161.0 %copy-start.6 = (bf16[512,1024]{0,1:T(8,128)(2,1)}, bf16[512,1024]{0,1:T(8,128)(2,1)S(1)}, u32[]{:S(2)}) copy-start(bf16[512,1024]{0,1:T(8,128)(2,1)S(1)} %copy.140) | copy-start | bytes 3145732
  33.4 132.8 %copy-start.17 = (f32[512,32]{0,1:T(8,128)}, f32[512,32]{0,1:T(8,128)S(1)}, u32[]{:S(2)}) copy-start(f32[512,32]{0,1:T(8,128)S(1)} %get-tuple-element.141) | copy-start | bytes 196612
  33.4 132.8 %copy-start.19 = (f32[512,32]{0,1:T(8,128)}, f32[512,32]{0,1:T(8,128)S(1)}, u32[]{:S(2)}) copy-start(f32[512,32]{0,1:T(8,128)S(1)} %get-tuple-element.142) | copy-start | bytes 196612
  33.7 118.5 %copy-start.43 = (f32[512]{0:T(512)}, f32[512]{0:T(512)S(1)}, u32[]{:S(2)}) copy-start(f32[512]{0:T(512)S(1)} %add_rsqrt_fusion.1) | copy-start | bytes 6148
  77.8 47.6 %collective-permute-start.5 = (bf16[256,1024]{1,0:T(8,128)(2,1)}, bf16[256,1024]{1,0:T(8,128)(2,1)S(1)}, u32[]{:S(2)}, u32[]{:S(2)}) collective-permute-start(bf16[256,1024]{1,0:T(8,128)(2,1)} %collective-permute-done.3), channel_id=1, source_target_pairs={{0,1},{1,2},{2,3},{3,0},{4,5},{5,6},{6,7},{7,4},{8,9},{9,10},{10,1... | collective-permute-start | bytes 1572872 | tf_op jit(solution)/shard_map/ppermute | solution.py:136
  90.9 57.7 %collective-permute-start.2 = (bf16[256,2176]{1,0:T(8,128)(2,1)}, bf16[256,2176]{1,0:T(8,128)(2,1)}, u32[]{:S(2)}, u32[]{:S(2)}) collective-permute-start(bf16[256,2176]{1,0:T(8,128)(2,1)} %collective-permute-done), channel_id=1, source_target_pairs={{0,1},{1,2},{2,3},{3,0},{4,5},{5,6},{6,7},{7,4},{8,9},{9,10},{10,1... | collective-permute-start | bytes 3342344 | tf_op jit(solution)/shard_map/ppermute | solution.py:136
  152.2 4.9 copy-start.40
  152.2 45.3 %copy-start.33 = (f32[1024,1]{0,1:T(1,128)}, f32[1024,1]{0,1:T(1,128)S(1)}, u32[]{:S(2)}) copy-start(f32[1024,1]{0,1:T(1,128)S(1)} %get-tuple-element.123) | copy-start | bytes 12292
  167.6 10.6 %copy-start.21 = (bf16[512,8,32]{0,2,1:T(8,128)(2,1)}, bf16[512,8,32]{0,2,1:T(8,128)(2,1)S(1)}, u32[]{:S(2)}) copy-start(bf16[512,8,32]{0,2,1:T(8,128)(2,1)S(1)} %get-tuple-element.137) | copy-start | bytes 786436
  167.6 10.6 %copy-start.23 = (bf16[512,8,32]{0,2,1:T(8,128)(2,1)}, bf16[512,8,32]{0,2,1:T(8,128)(2,1)S(1)}, u32[]{:S(2)}) copy-start(bf16[512,8,32]{0,2,1:T(8,128)(2,1)S(1)} %get-tuple-element.138) | copy-start | bytes 786436
  169.1 17.4 %copy-start.12 = (bf16[512,512]{0,1:T(8,128)(2,1)}, bf16[512,512]{0,1:T(8,128)(2,1)S(1)}, u32[]{:S(2)}) copy-start(bf16[512,512]{0,1:T(8,128)(2,1)S(1)} %copy.148) | copy-start | bytes 1572868
  178.2 8.3 copy-start.28
  186.5 7.6 copy-start.30
  194.1 5.0 copy-start.45
  197.5 5.5 copy-start.38
  199.0 59.4 %copy-start.4 = (bf16[512,1024]{0,1:T(8,128)(2,1)}, bf16[512,1024]{0,1:T(8,128)(2,1)S(1)}, u32[]{:S(2)}) copy-start(bf16[512,1024]{0,1:T(8,128)(2,1)S(1)} %multiply_convert_fusion.3) | copy-start | bytes 3145732
  199.1 28.1 %collective-permute-start.6 = (bf16[512,1024]{0,1:T(8,128)(2,1)S(1)}, bf16[512,1024]{0,1:T(8,128)(2,1)}, u32[]{:S(2)}, u32[]{:S(2)}) collective-permute-start(bf16[512,1024]{0,1:T(8,128)(2,1)S(1)} %multiply_convert_fusion.3), channel_id=1, source_target_pairs={{0,1},{1,2},{2,3},{3,0},{4,5},{5,6},{6,7},{7,4},{8,9},{9,10},{10,1... | collective-permute-start | bytes 3145736 | tf_op jit(solution)/shard_map/ppermute | solution.py:136
  199.1 53.6 %collective-permute-start.10 = (bf16[512,1152]{0,1:T(8,128)(2,1)}, bf16[512,1152]{0,1:T(8,128)(2,1)}, u32[]{:S(2)}, u32[]{:S(2)}) collective-permute-start(bf16[512,1152]{0,1:T(8,128)(2,1)} %get-tuple-element.139), channel_id=1, source_target_pairs={{0,3},{1,0},{2,1},{3,2},{4,7},{5,4},{6,5},{7,6},{8,11},{9,8},{10,9... | collective-permute-start | bytes 3538952 | tf_op jit(solution)/shard_map/ppermute | solution.py:144
  202.9 74.7 %collective-permute-start.11 = (bf16[512,1152]{0,1:T(8,128)(2,1)}, bf16[512,1152]{0,1:T(8,128)(2,1)S(1)}, u32[]{:S(2)}, u32[]{:S(2)}) collective-permute-start(bf16[512,1152]{0,1:T(8,128)(2,1)} %collective-permute-done.9), channel_id=1, source_target_pairs={{0,1},{1,2},{2,3},{3,0},{4,5},{5,6},{6,7},{7,4},{8,9},{9,10},{10,1... | collective-permute-start | bytes 3538952 | tf_op jit(solution)/shard_map/ppermute | solution.py:136
  202.9 94.0 %collective-permute-start.7 = (bf16[512,1024]{0,1:T(8,128)(2,1)S(1)}, bf16[512,1024]{0,1:T(8,128)(2,1)}, u32[]{:S(2)}, u32[]{:S(2)}) collective-permute-start(bf16[512,1024]{0,1:T(8,128)(2,1)S(1)} %multiply_convert_fusion.3), channel_id=1, source_target_pairs={{0,3},{1,0},{2,1},{3,2},{4,7},{5,4},{6,5},{7,6},{8,11},{9,8},{10,9... | collective-permute-start | bytes 3145736 | tf_op jit(solution)/shard_map/ppermute | solution.py:144
  227.1 93.8 %collective-permute-start.8 = (bf16[512,1024]{0,1:T(8,128)(2,1)}, bf16[512,1024]{0,1:T(8,128)(2,1)}, u32[]{:S(2)}, u32[]{:S(2)}) collective-permute-start(bf16[512,1024]{0,1:T(8,128)(2,1)} %collective-permute-done.6), channel_id=1, source_target_pairs={{0,1},{1,2},{2,3},{3,0},{4,5},{5,6},{6,7},{7,4},{8,9},{9,10},{10,1... | collective-permute-start | bytes 3145736 | tf_op jit(solution)/shard_map/ppermute | solution.py:136
  353.9 57.9 %copy-start.36 = (f32[4,2048]{1,0:T(4,128)}, f32[4,2048]{1,0:T(4,128)S(1)}, u32[]{:S(2)}) copy-start(f32[4,2048]{1,0:T(4,128)S(1)} %dynamic-slice_bitcast_fusion) | copy-start | bytes 98308
  411.8 163.0 %reduce-scatter.4.cloned.1.call-start = ((), (), s32[]{:S(2)}) async-start(), calls=%async_computation.3 | async-start | bytes 5242880 | tf_op jit(solution)/shard_map/reduce_scatter | solution.py:235
  425.9 70.1 %copy-start.2 = (f32[512,1024]{0,1:T(8,128)S(1)}, f32[512,1024]{0,1:T(8,128)}, u32[]{:S(2)}) copy-start(f32[512,1024]{0,1:T(8,128)} %copy-done.1) | copy-start | bytes 6291460
  425.9 70.1 %copy-start.34 = (f32[1024,1]{0,1:T(1,128)S(1)}, f32[1024,1]{0,1:T(1,128)}, u32[]{:S(2)}) copy-start(f32[1024,1]{0,1:T(1,128)} %copy-done.33) | copy-start | bytes 12292
  425.9 70.1 %copy-start.39 = (f32[512]{0:T(512)S(1)}, f32[512]{0:T(512)}, u32[]{:S(2)}) copy-start(f32[512]{0:T(512)} %copy-done.38) | copy-start | bytes 6148
  425.9 73.5 %copy-start.5 = (bf16[512,1024]{0,1:T(8,128)(2,1)S(1)}, bf16[512,1024]{0,1:T(8,128)(2,1)}, u32[]{:S(2)}) copy-start(bf16[512,1024]{0,1:T(8,128)(2,1)} %copy-done.4) | copy-start | bytes 3145732
  425.9 339.6 %reduce-scatter.8.cloned.1.call-start = ((), (), s32[]{:S(2)}) async-start(), calls=%async_computation.5 | async-start | bytes 8192000 | tf_op jit(solution)/shard_map/reduce_scatter | solution.py:333
  574.8 3.9 copy-start.46
  578.7 2.7 copy-start.9
  581.3 3.7 copy-start.13
  585.1 15.1 %slice-start = ((s8[16777216]{0:T(1024)(128)(4,1)}), s8[4194304]{0:T(1024)(128)(4,1)S(1)}, s32[]{:S(2)}) async-start(s8[16777216]{0:T(1024)(128)(4,1)} %bitcast.118), calls=%async_computation.7 | async-start | bytes 8388608
  585.1 15.1 %slice-start.1 = ((s8[16777216]{0:T(1024)(128)(4,1)}), s8[4194304]{0:T(1024)(128)(4,1)S(1)}, s32[]{:S(2)}) async-start(s8[16777216]{0:T(1024)(128)(4,1)} %bitcast.118), calls=%async_computation.8 | async-start | bytes 8388608
  585.1 15.1 %slice-start.2 = ((s8[16777216]{0:T(1024)(128)(4,1)}), s8[4194304]{0:T(1024)(128)(4,1)S(1)}, s32[]{:S(2)}) async-start(s8[16777216]{0:T(1024)(128)(4,1)} %bitcast.118), calls=%async_computation.9 | async-start | bytes 8388608
  585.1 16.4 %slice-start.3 = ((s8[16777216]{0:T(1024)(128)(4,1)}), s8[4194304]{0:T(1024)(128)(4,1)S(1)}, s32[]{:S(2)}) async-start(s8[16777216]{0:T(1024)(128)(4,1)} %bitcast.118), calls=%async_computation.10 | async-start | bytes 8388608
  585.1 16.4 %copy-start.27 = (f32[2,8,512]{2,1,0:T(8,128)S(1)}, f32[2,8,512]{2,1,0:T(8,128)}, u32[]{:S(2)}) copy-start(f32[2,8,512]{2,1,0:T(8,128)} %log_add_fusion) | copy-start | bytes 98308
  601.5 11.7 %copy-start.22 = (bf16[512,8,32]{0,2,1:T(8,128)(2,1)S(1)}, bf16[512,8,32]{0,2,1:T(8,128)(2,1)}, u32[]{:S(2)}) copy-start(bf16[512,8,32]{0,2,1:T(8,128)(2,1)} %copy-done.21) | copy-start | bytes 786436
  601.5 11.7 %copy-start.24 = (bf16[512,8,32]{0,2,1:T(8,128)(2,1)S(1)}, bf16[512,8,32]{0,2,1:T(8,128)(2,1)}, u32[]{:S(2)}) copy-start(bf16[512,8,32]{0,2,1:T(8,128)(2,1)} %copy-done.23) | copy-start | bytes 786436
  609.9 3.4 copy-start
  613.3 2.9 copy-start.14
  613.3 2.9 copy-start.15
  622.2 3.6 copy-start.18
  622.2 3.6 copy-start.20
  625.7 2.4 copy-start.7
  625.7 2.4 copy-start.25
  625.7 2.4 copy-start.41
  625.7 2.4 copy-start.44
  625.8 6.8 slice-start.4
  628.1 4.4 slice-start.5
  632.6 4.0 copy-start.32
  632.6 6.7 copy-start.16
  649.9 312.5 %all-reduce.3.cloned.1.call-start = ((), (), s32[]{:S(2)}) async-start(), calls=%async_computation.6 | async-start | bytes 28442624 | tf_op jit(solution)/shard_map/psum | solution.py:257
  962.5 1.9 copy-start.3
  (5 other events, 5.4 us)
Sparse Core Ops, SparseCore 0:
  411.9 83.2 reduce-scatter.5
  497.5 77.2 reduce-scatter.3
  650.0 115.4 reduce-scatter.7
  770.6 191.8 all-reduce.2
